TPU v7x, 32 devices: a whole 2x2x4 slice. The times are simulated.
32 devices in a mesh: grp: 4 (over y, x), tok: 8 (over z, core).
Axes of the slice: x: 2, y: 2, z: 4, core: 2. Of those that a mesh axis runs over, the one named last changes fastest.
Arguments:
- tokens_in: bfloat16 [32768, 768], P(('grp', 'tok')), may hold values from -6 to 6
- w_qkv: bfloat16 [768, 2304], replicated, may hold values from -0.3125 to 0.3125
- b_query: bfloat16 [768], replicated, may hold values from -3 to 3
- b_value: bfloat16 [768], replicated, may hold values from -3 to 3
- w_out: bfloat16 [768, 768], replicated, may hold values from -0.875 to 0.875
- b_out: bfloat16 [768], replicated, may hold values from -3 to 3
- norm1_gain: bfloat16 [768], replicated, may hold values from 0.5 to 1.5
- norm1_shift: bfloat16 [768], replicated, may hold values from -2 to 2
- w_up: bfloat16 [768, 3072], replicated, may hold values from -0.21875 to 0.21875
- b_up: bfloat16 [3072], replicated, may hold values from -3 to 3
- w_down: bfloat16 [3072, 768], replicated, may hold values from -0.109375 to 0.109375
- b_down: bfloat16 [768], replicated, may hold values from -3 to 3
- norm2_gain: bfloat16 [768], replicated, may hold values from 0.5 to 1.5
- norm2_shift: bfloat16 [768], replicated, may hold values from -2 to 2
- out_grad: bfloat16 [32768, 768], P(('grp', 'tok')), may hold values from -6 to 6
- doc_lengths: int32 [4, 5], P('grp'), may hold values from 1 to 7680, as said below
- cluster_slots: int32 [32768], P(('grp', 'tok')), may hold values from 0 to 8191, as said below
Outputs:
- block_out: bfloat16 [32768, 768], P(('grp', 'tok'))
- grad_tokens: bfloat16 [32768, 768], P(('grp', 'tok'))
- grad_w_qkv: float32 [768, 2304], P('tok')
- grad_b_query: float32 [768], P('tok')
- grad_b_value: float32 [768], P('tok')
- grad_w_out: float32 [768, 768], P('tok')
- grad_b_out: float32 [768], P('tok')
- grad_norm1_gain: float32 [768], P('tok')
- grad_norm1_shift: float32 [768], P('tok')
- grad_w_up: float32 [768, 3072], P('tok')
- grad_b_up: float32 [3072], P('tok')
- grad_w_down: float32 [3072, 768], P('tok')
- grad_b_down: float32 [768], P('tok')
- grad_norm2_gain: float32 [768], P('tok')
- grad_norm2_shift: float32 [768], P('tok')
Inputs may be any that keep to these rules, and one draw needn't show every extreme that they name: `doc_lengths`: in each group the documents, each padded up to a multiple of 128 rows, fill the group's rows exactly; one document of each group has the full length and spans from the group's first device to its last. `cluster_slots`: within each group the slots are a permutation of 0 to the group's rows - 1; the rows of every device of a group go to the slot range s // 1024 of every device of the group in equal numbers, 1024 / 8 each.
All inputs are finite; a program needn't handle non-finite values.
Results may differ from a plain program's by a relative error of at most 0.017.
The roundings to bfloat16 on the way count: a program that leaves them out, or rounds other values in their place, can miss the bound.
Values may be sent and summed in bfloat16 or wider, within the bound.
A program may use at most 192 MiB of HBM per device.

v0:
```python
import functools

import jax
import jax.numpy as jnp
from jax import lax
from jax.experimental import pallas as pl
from jax.experimental.pallas import tpu as pltpu
from jax.sharding import PartitionSpec as P

H = 12
CLU = 128

eps = 1e-12
masked_score = -1000000000.0

MESH = pl.DeviceIdType.MESH
f32 = jnp.float32
bf16 = jnp.bfloat16
BLK = 256


def dot32(a, b):
    return jnp.dot(a, b, preferred_element_type=jnp.float32)


def dot_rows(a, b):
    return lax.dot_general(a, b, (((1,), (1,)), ((), ())), preferred_element_type=jnp.float32)


def dot_cols(a, b):
    return lax.dot_general(a, b, (((0,), (0,)), ((), ())), preferred_element_type=jnp.float32)


def peer_order(n_tok):
    return sorted(range(1, n_tok), key=lambda k: -k)


def row_of(ref):
    return ref[...].astype(f32)[None, :]


def norm_parts(values):
    centre = values - jnp.mean(values, axis=-1, keepdims=True)
    spread = jnp.mean(centre * centre, axis=-1, keepdims=True)
    rstd = lax.rsqrt(spread + eps)
    return centre * rstd, rstd


def lane_halves(width):
    lane = lax.broadcasted_iota(jnp.int32, (1, width), 1)
    low = (lane < width // 2).astype(f32)
    return low.astype(bf16), (1.0 - low).astype(bf16)


def stack_heads(pair, halves):
    return jnp.concatenate([pair * halves[0], pair * halves[1]], axis=0)


def one_over_other(pair):
    half = pair.shape[1] // 2
    return jnp.concatenate([pair[:, :half], pair[:, half:]], axis=0)


def column_of(row):
    amount = row.shape[1]
    return jnp.concatenate(
        [
            jnp.broadcast_to(row[:, at : at + 128], (128, 128)).T
            for at in range(0, amount, 128)
        ],
        axis=0,
    )


def hot_from_column(column, amount):
    lane = lax.broadcasted_iota(jnp.int32, column.shape, 1).astype(f32)
    return jnp.concatenate(
        [(lane + float(at) == column).astype(f32).astype(bf16) for at in range(0, amount, 128)],
        axis=1,
    )


def forward_kernel(
    n_tok, per,
    slots_ref, docs_ref, tok_ref, og_ref, wq_ref, bq_ref, bv_ref, wo_ref, bo_ref, g1_ref, s1_ref,
    wu_ref, bu_ref, wd_ref, bd_ref, g2_ref, s2_ref,
    xc_o, gc_o, qkv_o, p_o, ctx_o, r1_o, n1_o, gelu_o, gelup_o, r2_o, back_o, col_o, pos_o,
    xh, gh, xs, gs, xr, gr, hot, note_s, note_r, wq, wo, wu, wd, live_s,
    xc_t, qkv_t, p_t, ctx_t, r1_t, n1_t, gelu_t, gelup_t, r2_t, bo_c, back_t, gc_t, col_t, pos_t,
    load_sem, note_ss, note_rs, x_ss, x_rs, g_ss, g_rs, own_sem, out_sem, last_sem,
):
    rows, width = xh.shape
    ffw = wu.shape[1]
    blocks = rows // BLK
    grp = lax.axis_index("grp")
    me = lax.axis_index("tok")
    order = peer_order(n_tok)

    barrier = pltpu.get_barrier_semaphore()
    for k in order:
        pl.semaphore_signal(barrier, inc=1, device_id=(grp, me ^ k), device_id_type=MESH)

    loads = [
        pltpu.make_async_copy(src, dst, load_sem.at[i])
        for i, (src, dst) in enumerate(
            ((tok_ref, xh), (og_ref, gh), (wq_ref, wq), (wo_ref, wo), (wu_ref, wu), (wd_ref, wd))
        )
    ]
    loads[0].start()

    def note_copy(k):
        return pltpu.make_async_remote_copy(
            src_ref=note_s.at[me ^ k], dst_ref=note_r.at[me], send_sem=note_ss.at[k],
            recv_sem=note_rs.at[k], device_id=(grp, me ^ k), device_id_type=MESH,
        )

    def row_copy(src, dst, ss, rs, k):
        return pltpu.make_async_remote_copy(
            src_ref=src.at[pl.ds(pl.multiple_of((me ^ k) * per, per), per)],
            dst_ref=dst.at[pl.ds(pl.multiple_of(me * per, per), per)],
            send_sem=ss.at[k], recv_sem=rs.at[k], device_id=(grp, me ^ k), device_id_type=MESH,
        )

    slots = slots_ref[...][None, :]
    dest = jnp.right_shift(slots, rows.bit_length() - 1)
    within = jnp.bitwise_and(slots, rows - 1)
    lanes = lax.broadcasted_iota(jnp.int32, (1, rows), 1)
    dest_hot = lax.broadcasted_iota(jnp.int32, (16, rows), 0) == dest
    dest_hot = dest_hot.astype(f32)
    before = lax.broadcasted_iota(jnp.int32, (BLK, rows), 1)
    rank = jnp.zeros((16, rows), f32)
    for b in range(blocks):
        earlier = lax.broadcasted_iota(jnp.int32, (BLK, rows), 0) + b * BLK < before
        rank += dot32(
            dest_hot[:, b * BLK : (b + 1) * BLK].astype(bf16), earlier.astype(f32).astype(bf16)
        )
    rank = jnp.sum(rank * dest_hot, axis=0, keepdims=True).astype(jnp.int32)
    pos = dest * per + rank
    spot = lax.broadcasted_iota(jnp.int32, (BLK, rows), 0)
    chip = lax.div(me * per, BLK)
    loads[0].wait()
    for copy in loads[1:]:
        copy.start()
    for j in range(blocks - 1, -1, -1):
        at = pl.multiple_of((chip ^ j) * BLK, BLK)
        picked = (spot + at == pos).astype(f32).astype(bf16)
        hot[pl.ds(at, BLK), :] = picked
        xs[pl.ds(at, BLK), :] = dot32(picked, xh[...]).astype(bf16)
        if j == blocks - 1:
            pl.semaphore_wait(barrier, n_tok - 1)
        for k in order:
            if k // (BLK // per) == j:
                row_copy(xs, xr, x_ss, x_rs, k).start()
    mine = pl.ds(pl.multiple_of(me * per, per), per)
    own_x = pltpu.make_async_copy(xs.at[mine], xr.at[mine], own_sem.at[0])
    own_x.start()

    pos_t[...] = jnp.broadcast_to(pos, (8, rows))
    start = jnp.int32(0)
    position = lanes + me * rows
    usable = jnp.zeros((1, rows), jnp.int32)
    for i in range(docs_ref.shape[1]):
        length = docs_ref[0, i]
        inside = (position >= start) & (position < start + length)
        usable = jnp.where(inside, 1, usable)
        start = start + jnp.bitwise_and(length + (CLU - 1), -CLU)
    kind = lax.broadcasted_iota(jnp.int32, (16, rows), 0)
    notes = jnp.where(
        kind == 0,
        jnp.right_shift(within, 5),
        jnp.where(kind == 1, jnp.bitwise_and(within, 31), jnp.where(kind == 2, usable, 0)),
    )
    notes = dot_rows(notes.astype(f32).astype(bf16), hot[...]).astype(bf16)
    for d in range(n_tok):
        note_s[d] = notes[:, d * per : (d + 1) * per]
    for k in order:
        note_copy(k).start()
    own_note = pltpu.make_async_copy(note_s.at[me], note_r.at[me], own_sem.at[1])
    own_note.start()
    loads[1].wait()
    for b in range(blocks):
        sl = pl.ds(b * BLK, BLK)
        gs[sl, :] = dot32(hot[sl, :], gh[...]).astype(bf16)
    own_g = pltpu.make_async_copy(gs.at[mine], gr.at[mine], own_sem.at[2])
    own_g.start()

    own_note.wait()
    for k in order:
        note_copy(k).wait_recv()
    got = jnp.concatenate([note_r[d] for d in range(n_tok)], axis=1)
    got32 = got.astype(f32)
    slot_row = got32[0:1, :] * 32.0 + got32[1:2, :]
    col_t[...] = column_of(slot_row)
    slot_row = slot_row.astype(jnp.int32)
    for b in range(blocks):
        spot = lax.broadcasted_iota(jnp.int32, (BLK, rows), 0) + b * BLK
        hot[b * BLK : (b + 1) * BLK, :] = (spot == slot_row).astype(f32).astype(bf16)
    live_s[...] = column_of(dot_rows(got, hot[...])[2:3, :])

    def gather_rows(source, target, own, copy):
        for j in range(blocks):
            if j == 0:
                own.wait()
            for k in range(1, n_tok):
                if k // (BLK // per) == j:
                    copy(k).wait_recv()
            at = pl.multiple_of((chip ^ j) * BLK, BLK)
            for b in range(blocks):
                sl = pl.ds(b * BLK, BLK)
                part = dot32(hot[sl, pl.ds(at, BLK)], source[pl.ds(at, BLK), :]).astype(bf16)
                target[sl, :] = part if j == 0 else target[sl, :] + part

    for k in order:
        row_copy(xs, xr, x_ss, x_rs, k).wait_send()
    for k in order:
        row_copy(gs, gr, g_ss, g_rs, k).start()
    gather_rows(xr, xc_t, own_x, lambda k: row_copy(xs, xr, x_ss, x_rs, k))
    xc_out = pltpu.make_async_copy(xc_t, xc_o, last_sem.at[4])
    xc_out.start()
    for copy in loads[2:]:
        copy.wait()

    halves = lane_halves(2 * width // H)
    pair_width = 2 * width // H
    scale = (width // H) ** (-0.5)
    outs = (
        (qkv_t, qkv_o, BLK), (p_t, p_o, BLK * H // 2), (ctx_t, ctx_o, BLK), (r1_t, r1_o, BLK),
        (n1_t, n1_o, BLK), (gelu_t, gelu_o, BLK), (gelup_t, gelup_o, BLK), (r2_t, r2_o, BLK),
    )

    def out_copy(i, b, slot):
        tile, whole, count = outs[i]
        return pltpu.make_async_copy(
            tile.at[slot], whole.at[pl.ds(pl.multiple_of(b * count, count), count)], out_sem.at[slot, i]
        )

    def block(b, carry):
        slot = lax.rem(b, 2)
        sl = pl.ds(pl.multiple_of(b * BLK, BLK), BLK)

        @pl.when(b >= 2)
        def _():
            for i in range(len(outs)):
                out_copy(i, b - 2, slot).wait()

        x = xc_t[sl, :]
        for part, bias in ((0, row_of(bq_ref)), (1, None), (2, row_of(bv_ref))):
            got_part = dot32(x, wq[:, part * width : (part + 1) * width])
            if bias is not None:
                got_part = got_part + bias
            qkv_t[slot, :, part * width : (part + 1) * width] = got_part.astype(bf16)
        for c in range(BLK // CLU):
            at = pl.multiple_of(b * BLK + c * CLU, CLU)
            live = live_s[pl.ds(at, CLU), :] > 0.5
            live = jnp.concatenate([live, live], axis=1)
            crow = pl.ds(c * CLU, CLU)
            for p in range(H // 2):
                cols = [pl.ds(part * width + p * pair_width, pair_width) for part in range(3)]
                q2 = stack_heads(qkv_t[slot, crow, cols[0]], halves)
                k2 = qkv_t[slot, crow, cols[1]]
                v2 = stack_heads(qkv_t[slot, crow, cols[2]], halves)
                scores = jnp.where(live, dot_rows(k2, q2) * scale, masked_score)
                expo = jnp.exp(scores - jnp.max(scores, axis=0, keepdims=True))
                weights = (expo / jnp.sum(expo, axis=0, keepdims=True)).astype(bf16)
                p_t[slot, pl.ds((c * (H // 2) + p) * CLU, CLU), :] = weights
                context = dot_cols(one_over_other(weights), v2)
                ctx_t[slot, crow, pl.ds(p * pair_width, pair_width)] = context.astype(bf16)
        resid1 = x.astype(f32) + (dot32(ctx_t[slot], wo[...]) + row_of(bo_ref))
        r1_t[slot] = resid1
        hat1, _ = norm_parts(resid1)
        normed1 = hat1 * row_of(g1_ref) + row_of(s1_ref)
        low1 = normed1.astype(bf16)
        n1_t[slot] = low1
        down = None
        step = width
        for j in range(ffw // step):
            cs = pl.ds(j * step, step)
            up = dot32(low1, wu[:, cs]) + bu_ref[cs].astype(f32)[None, :]
            phi = 0.5 * (1.0 + lax.erf(up * 0.7071067811865476))
            slope = phi + up * jnp.exp(up * up * -0.5) * 0.3989422804014327
            act = (up * phi).astype(bf16)
            gelu_t[slot, :, cs] = act
            gelup_t[slot, :, cs] = slope.astype(bf16)
            term = dot32(act, wd[cs, :])
            down = term if down is None else down + term
        resid2 = normed1 + (down + row_of(bd_ref))
        r2_t[slot] = resid2
        hat2, _ = norm_parts(resid2)
        bo_c[sl, :] = (hat2 * row_of(g2_ref) + row_of(s2_ref)).astype(bf16)
        for i in range(len(outs)):
            out_copy(i, b, slot).start()
        return carry

    lax.fori_loop(0, blocks, block, 0)

    col_out = pltpu.make_async_copy(col_t, col_o, last_sem.at[0])
    col_out.start()
    pos_out = pltpu.make_async_copy(pos_t, pos_o, last_sem.at[1])
    pos_out.start()
    for b in range(blocks):
        sl = pl.ds(b * BLK, BLK)
        back_t[sl, :] = dot32(hot_from_column(col_t[sl, :], rows), bo_c[...]).astype(bf16)
    back_out = pltpu.make_async_copy(back_t, back_o, last_sem.at[2])
    back_out.start()
    gather_rows(gr, gc_t, own_g, lambda k: row_copy(gs, gr, g_ss, g_rs, k))
    gc_out = pltpu.make_async_copy(gc_t, gc_o, last_sem.at[3])
    gc_out.start()
    for k in order:
        note_copy(k).wait_send()
        row_copy(gs, gr, g_ss, g_rs, k).wait_send()
    for b in range(max(blocks - 2, 0), blocks):
        for i in range(len(outs)):
            out_copy(i, b, b % 2).wait()
    col_out.wait()
    pos_out.wait()
    back_out.wait()
    gc_out.wait()
    xc_out.wait()


def forward(n_tok, tokens_in, w_qkv, b_query, b_value, w_out, b_out, norm1_gain, norm1_shift,
            w_up, b_up, w_down, b_down, norm2_gain, norm2_shift, out_grad, doc_lengths, cluster_slots):
    rows, width = tokens_in.shape
    ffw = w_up.shape[1]
    per = rows // n_tok
    vm = pl.BlockSpec(memory_space=pltpu.VMEM)
    sm = pl.BlockSpec(memory_space=pltpu.SMEM)
    hb = pl.BlockSpec(memory_space=pl.ANY)
    out_shape = [
        ((rows, width), bf16), ((rows, width), bf16), ((rows, 3 * width), bf16), ((rows * H // 2, 2 * CLU), bf16),
        ((rows, width), bf16), ((rows, width), f32), ((rows, width), bf16), ((rows, ffw), bf16),
        ((rows, ffw), bf16), ((rows, width), f32), ((rows, width), bf16), ((rows, 128), f32),
        ((8, rows), jnp.int32),
    ]
    vmem = pltpu.VMEM
    dma = pltpu.SemaphoreType.DMA
    scratch = (
        [vmem((rows, width), bf16)] * 6
        + [vmem((rows, rows), bf16), vmem((n_tok, 16, per), bf16), vmem((n_tok, 16, per), bf16)]
        + [vmem(w_qkv.shape, bf16), vmem(w_out.shape, bf16), vmem(w_up.shape, bf16), vmem(w_down.shape, bf16)]
        + [vmem((rows, 128), f32)]
        + [
            vmem((rows, width), bf16), vmem((2, BLK, 3 * width), bf16), vmem((2, BLK * H // 2, 2 * CLU), bf16),
            vmem((2, BLK, width), bf16), vmem((2, BLK, width), f32), vmem((2, BLK, width), bf16),
            vmem((2, BLK, ffw), bf16), vmem((2, BLK, ffw), bf16), vmem((2, BLK, width), f32),
            vmem((rows, width), bf16), vmem((rows, width), bf16), vmem((rows, width), bf16),
            vmem((rows, 128), f32), vmem((8, rows), jnp.int32),
        ]
        + [dma((6,))] + [dma((n_tok,))] * 6 + [dma((3,)), dma((2, 8)), dma((5,))]
    )
    return pl.pallas_call(
        functools.partial(forward_kernel, n_tok, per),
        out_shape=[jax.ShapeDtypeStruct(s, d) for s, d in out_shape],
        in_specs=[vm, sm, hb, hb, hb, vm, vm, hb, vm, vm, vm, hb, vm, hb, vm, vm, vm],
        out_specs=[hb] * len(out_shape),
        scratch_shapes=scratch,
        compiler_params=pltpu.CompilerParams(
            collective_id=0, has_side_effects=True, vmem_limit_bytes=60 * 2**20
        ),
        name="layer_forward",
    )(cluster_slots, doc_lengths, tokens_in, out_grad, w_qkv, b_query, b_value, w_out, b_out, norm1_gain,
      norm1_shift, w_up, b_up, w_down, b_down, norm2_gain, norm2_shift)


def grad_kinds(width, ffw, n_tok):
    return ((ffw // n_tok, width), (width // n_tok, ffw), (width // n_tok, width), (width // n_tok, 3 * width))


def backward_kernel(n_tok, per, kinds, *refs):
    (xc_ref, gc_ref, qkv_ref, p_ref, ctx_ref, r1_ref, n1_ref, gelu_ref, gelup_ref, r2_ref, back_ref, col_ref,
     wq_ref, wo_ref, wu_ref, wd_ref, g1_ref, g2_ref) = refs[:18]
    refs = refs[18:]
    bo_got, gt_got, nar_o = refs[:3]
    shares = refs[3:7]
    refs = refs[7:]
    (wq, wo, wu, wd, gwd, gelu, gup, low1, gdown, resid, grow, ctx, gattn, gcl, qkv, probs, land0, col,
     nar_v, bup_v, nar_s, nar_r, nar_g, nar_h, nar_t,
     load_sem, bo_ss, bo_rs, gt_ss, gt_rs, own_sem, s0_ss, s0_rs, x1_ss, x1_rs, x2_ss, x2_rs, za_ss, za_rs,
     zb_ss, zb_rs, ag_ss, ag_rs, fin_sem, free_sem, nt_ss, nt_rs, ng_ss, ng_rs) = refs
    rows, width = low1.shape
    ffw = wu.shape[1]
    blocks = rows // BLK
    grp = lax.axis_index("grp")
    me = lax.axis_index("tok")
    core = lax.rem(me, 2)
    chip = lax.div(me, 2)
    chips = n_tok // 2
    gx = lax.rem(grp, 2)
    gy = lax.div(grp, 2)
    order = peer_order(n_tok)
    mats = (gwd, wu, wo, wq)

    barrier = pltpu.get_barrier_semaphore()
    for k in order:
        pl.semaphore_signal(barrier, inc=1, device_id=(grp, me ^ k), device_id_type=MESH)
    for k in (1, 2, 3):
        pl.semaphore_signal(barrier, inc=1, device_id=(grp ^ k, me), device_id_type=MESH)

    load = {
        name: pltpu.make_async_copy(src, dst, load_sem.at[i])
        for i, (name, src, dst) in enumerate((
            ("gc", gc_ref, gcl), ("r2", r2_ref, resid), ("gelu", gelu_ref, gelu), ("wd", wd_ref, wd),
            ("gelup", gelup_ref, gup), ("wu", wu_ref, wu), ("n1", n1_ref, low1), ("wo", wo_ref, wo),
            ("ctx", ctx_ref, ctx), ("qkv", qkv_ref, qkv), ("p", p_ref, probs), ("wq", wq_ref, wq),
            ("xc", xc_ref, gattn), ("col", col_ref, col), ("r1", r1_ref, resid),
        ))
    }

    def begin(*names):
        for name in names:
            load[name].start()

    def ready(*names):
        for name in names:
            load[name].wait()

    begin("gc", "r2")

    def row_copy(src, dst, ss, rs, k):
        return pltpu.make_async_remote_copy(
            src_ref=src.at[pl.ds(pl.multiple_of((me ^ k) * per, per), per)],
            dst_ref=dst.at[pl.ds(pl.multiple_of(me * per, per), per)],
            send_sem=ss.at[k], recv_sem=rs.at[k], device_id=(grp, me ^ k), device_id_type=MESH,
        )

    mine = pl.ds(pl.multiple_of(me * per, per), per)
    def held(m, z, row0, count, col0, ncols):
        share, _ = kinds[m]
        at = (2 * z + core) * share + row0
        return mats[m].at[pl.ds(pl.multiple_of(at, 16), count), pl.ds(pl.multiple_of(col0, 128), ncols)]

    zones = (land0, gelu, gup, gup)
    zone_col = (0, 0, 3 * width, 0)

    def land(m, row, count, half_at, whole):
        share, cols = kinds[m]
        ncols = cols if whole else cols // 2
        return zones[m].at[pl.ds(row, count), pl.ds(zone_col[m] + half_at * (cols // 2), ncols)]

    def land_s0(m, z):
        share = kinds[m][0]
        return land(m, z * share, share, 0, True)

    def land_x1(m, z):
        share = kinds[m][0]
        if first_x(z):
            return land(m, (chips + z) * share, share, 0, False)
        return land(m, (chips + 2) * share + (z - chips // 2) * (share // 2), share // 2, 0, True)

    def land_x2(m, z):
        share = kinds[m][0]
        return land(m, chips * share + z * (share // 2), share // 2, 1, False)

    def land_za(m, i):
        share = kinds[m][0]
        return land(m, (chips + 3) * share, share // 2, i, False)

    def land_zb(m):
        share = kinds[m][0]
        return land(m, (chips + 3) * share + share // 2, share // 2, 0, False)

    partners = ((grp, me ^ 1), (grp ^ 1, me), (grp ^ 2, me), (grp, me ^ 2), (grp, me ^ 4))

    def tell_free(i):
        for who in partners:
            pl.semaphore_signal(free_sem.at[i], inc=1, device_id=who, device_id_type=MESH)

    def partners_free(i):
        pl.semaphore_wait(free_sem.at[i], len(partners))

    def remote(src, dst, ss, rs, who):
        return pltpu.make_async_remote_copy(
            src_ref=src, dst_ref=dst, send_sem=ss, recv_sem=rs, device_id=who, device_id_type=MESH
        )

    def copy_s0(m, z):
        share, cols = kinds[m]
        at = (2 * z + 1 - core) * share
        return remote(
            mats[m].at[pl.ds(pl.multiple_of(at, 16), share)], land_s0(m, z),
            s0_ss.at[m, z], s0_rs.at[m, z], (grp, me ^ 1),
        )

    def first_x(z):
        return z < chips // 2

    def copy_x1(m, z):
        share, cols = kinds[m]
        half, hcols = share // 2, cols // 2
        if first_x(z):
            src = held(m, z, 0, share, (1 - gx) * hcols, hcols)
            who = (grp ^ 1, me)
        else:
            src = held(m, z, (1 - gy) * half, half, 0, cols)
            who = (grp ^ 2, me)
        return remote(src, land_x1(m, z), x1_ss.at[m, z], x1_rs.at[m, z], who)

    def copy_x2(m, z):
        share, cols = kinds[m]
        half, hcols = share // 2, cols // 2
        if first_x(z):
            src, who = held(m, z, (1 - gy) * half, half, gx * hcols, hcols), (grp ^ 2, me)
        else:
            src, who = held(m, z, gy * half, half, (1 - gx) * hcols, hcols), (grp ^ 1, me)
        return remote(src, land_x2(m, z), x2_ss.at[m, z], x2_rs.at[m, z], who)

    def quarter(m, z):
        share, cols = kinds[m]
        half, hcols = share // 2, cols // 2
        return held(m, z, gy * half, half, gx * hcols, hcols)

    def copy_za(m, i):
        return remote(quarter(m, chip ^ (1 + 2 * i)), land_za(m, i), za_ss.at[m, i], za_rs.at[m, i], (grp, me ^ 2))

    def copy_zb(m):
        return remote(quarter(m, chip ^ 2), land_zb(m), zb_ss.at[m], zb_rs.at[m], (grp, me ^ 4))

    def share_part(m):
        share, cols = kinds[m]
        half, hcols = share // 2, cols // 2
        return shares[m].at[
            pl.ds(pl.multiple_of(gy * half, 16), half), pl.ds(pl.multiple_of(gx * hcols, 128), hcols)
        ]

    def own_part(m):
        return quarter(m, chip)

    def copy_ag(m, k):
        return remote(own_part(m), share_part(m), ag_ss.at[m, k], ag_rs.at[m, k], (grp ^ k, me))

    def own_ag(m):
        return pltpu.make_async_copy(own_part(m), share_part(m), fin_sem.at[m])

    def add_in(target, extra):
        target[...] = target[...] + extra[...]

    def start_s0(m):
        for z in range(chips):
            copy_s0(m, z).start()

    def step_r0(m, zs=None):
        share, cols = kinds[m]
        for z in zs or range(chips):
            copy_s0(m, z).wait_recv()
            add_in(held(m, z, 0, share, 0, cols), land_s0(m, z))
            copy_x1(m, z).start()

    def step_r1(m):
        share, cols = kinds[m]
        half, hcols = share // 2, cols // 2
        for z in range(chips):
            copy_x1(m, z).wait_recv()
            spot = (0, share, gx * hcols, hcols) if first_x(z) else (gy * half, half, 0, cols)
            add_in(held(m, z, *spot), land_x1(m, z))
            copy_x2(m, z).start()

    def step_r2(m):
        for z in range(chips):
            copy_x2(m, z).wait_recv()
            add_in(quarter(m, z), land_x2(m, z))
        copy_za(m, 0).start()
        copy_za(m, 1).start()

    def step_ra(m):
        copy_za(m, 0).wait_recv()
        copy_za(m, 1).wait_recv()
        add_in(quarter(m, chip ^ 2), land_za(m, 1))
        copy_zb(m).start()
        add_in(own_part(m), land_za(m, 0))

    def step_rb(m):
        copy_zb(m).wait_recv()
        add_in(own_part(m), land_zb(m))
        for k in (3, 1, 2):
            copy_ag(m, k).start()
        own_ag(m).start()

    gain2 = row_of(g2_ref)
    gain1 = row_of(g1_ref)

    def norm_back(upstream, resid_rows, gain):
        hat, rstd = norm_parts(resid_rows)
        dh = upstream * gain
        inner = jnp.mean(dh * hat, axis=-1, keepdims=True)
        return rstd * (dh - jnp.mean(dh, axis=-1, keepdims=True) - hat * inner), hat

    def add_sum(at, values):
        nar_v[at : at + 1, :] += jnp.sum(values, axis=0, keepdims=True)

    nar_v[...] = jnp.zeros_like(nar_v)
    bup_v[...] = jnp.zeros_like(bup_v)
    own_bo = pltpu.make_async_copy(back_ref.at[mine], bo_got.at[mine], own_sem.at[0])
    ready("gc", "r2")
    begin("gelu", "wd", "gelup")
    for b in range(blocks):
        sl = pl.ds(b * BLK, BLK)
        g = gcl[sl, :].astype(f32)
        back, hat = norm_back(g, resid[sl, :], gain2)
        low = back.astype(bf16)
        grow[sl, :] = back
        gdown[sl, :] = low
        add_sum(5, low.astype(f32))
        add_sum(6, g * hat)
        add_sum(7, g)
        if b == 0:
            pl.semaphore_wait(barrier, n_tok - 1 + 3)
            for k in order:
                row_copy(back_ref, bo_got, bo_ss, bo_rs, k).start()
            own_bo.start()

    ready("gelu")
    begin("wu", "r1", "wo", "n1", "ctx")
    step = width
    for j in range(ffw // step):
        cs = pl.ds(j * step, step)
        gwd[cs, :] = dot_cols(gelu[:, cs], gdown[...]).astype(bf16)
        if step == 2 * kinds[0][0]:
            copy_s0(0, j).start()
    if step != 2 * kinds[0][0]:
        start_s0(0)
    tell_free(0)
    ready("wd", "gelup")
    for b in range(blocks):
        sl = pl.ds(b * BLK, BLK)
        for j in range(ffw // step):
            cs = pl.ds(j * step, step)
            up = (dot_rows(gdown[sl, :], wd[cs, :]) * gup[sl, cs].astype(f32)).astype(bf16)
            gup[sl, cs] = up
            bup_v[0:1, cs] += jnp.sum(up.astype(f32), axis=0, keepdims=True)
        if b == 1:
            step_r0(0, (0, 1))
    step_r0(0, (2, 3))
    begin("qkv", "p", "wq", "col")
    ready("wu", "r1", "wo")
    for b in range(blocks):
        sl = pl.ds(b * BLK, BLK)
        gn1 = grow[sl, :] + dot_rows(gup[sl, :], wu[...])
        back, hat = norm_back(gn1, resid[sl, :], gain1)
        low = back.astype(bf16)
        grow[sl, :] = back
        gattn[sl, :] = low
        add_sum(2, low.astype(f32))
        add_sum(3, gn1 * hat)
        add_sum(4, gn1)
        gcl[sl, :] = dot_rows(low, wo[...]).astype(bf16)
    ready("n1")
    for j in range(ffw // step):
        cs = pl.ds(j * step, step)
        wu[:, cs] = dot_cols(low1[...], gup[:, cs]).astype(bf16)
    tell_free(1)
    partners_free(0)
    start_s0(1)
    ready("ctx")
    wo[...] = dot_cols(ctx[...], gattn[...]).astype(bf16)
    begin("xc")
    partners_free(1)
    start_s0(2)
    step_r1(0)

    ready("qkv", "p", "wq")
    halves = lane_halves(2 * width // H)
    pair_width = 2 * width // H
    scale = (width // H) ** (-0.5)

    def attend(b):
        for c in range(BLK // CLU):
            crow = pl.ds(b * BLK + c * CLU, CLU)
            for p in range(H // 2):
                cols = [pl.ds(part * width + p * pair_width, pair_width) for part in range(3)]
                q2 = stack_heads(qkv[crow, cols[0]], halves)
                k2 = stack_heads(qkv[crow, cols[1]], halves)
                v2 = qkv[crow, cols[2]]
                go = stack_heads(gcl[crow, pl.ds(p * pair_width, pair_width)], halves)
                weights = probs[pl.ds(((b * BLK // CLU + c) * (H // 2) + p) * CLU, CLU), :]
                weights32 = weights.astype(f32)
                gp = dot_rows(v2, go)
                dot = jnp.sum(gp * weights32, axis=0, keepdims=True)
                gs = (weights32 * (gp - dot)).astype(bf16)
                gq = (dot_cols(one_over_other(gs), k2) * scale).astype(bf16)
                gk = (dot32(gs, q2) * scale).astype(bf16)
                gv = dot32(weights, go).astype(bf16)
                qkv[crow, cols[0]] = gq
                qkv[crow, cols[1]] = gk
                qkv[crow, cols[2]] = gv
        sl = pl.ds(b * BLK, BLK)
        add_sum(0, qkv[sl, 0:width].astype(f32))
        add_sum(1, qkv[sl, 2 * width :].astype(f32))
        total = grow[sl, :] + dot_rows(qkv[sl, :], wq[...])
        low1[sl, :] = total.astype(bf16)

    attend(0)
    attend(1)
    step_r0(1)
    step_r0(2)
    attend(2)
    step_r2(0)
    attend(3)
    ready("xc", "col")
    for j in range(3):
        cs = pl.ds(j * step, step)
        wq[:, cs] = dot_cols(gattn[...], qkv[:, cs]).astype(bf16)
    start_s0(3)
    for b in range(blocks):
        sl = pl.ds(b * BLK, BLK)
        gdown[sl, :] = dot32(hot_from_column(col[sl, :], rows), low1[...]).astype(bf16)
    for k in order:
        row_copy(gdown, gt_got, gt_ss, gt_rs, k).start()
    own_gt = pltpu.make_async_copy(gdown.at[mine], gt_got.at[mine], own_sem.at[1])
    own_gt.start()
    step_ra(0)
    step_r0(3)
    step_r1(1)
    step_r1(2)

    each = width // n_tok
    at = lax.broadcasted_iota(jnp.int32, (width, n_tok * 128), 0)
    lane = lax.broadcasted_iota(jnp.int32, (width, n_tok * 128), 1)
    inner = jnp.bitwise_and(lane, 127)
    pick = (at == jnp.right_shift(lane, 7) * each + inner) & (inner < each)
    spread = jnp.dot(nar_v[...], pick.astype(f32), precision=lax.Precision.HIGHEST, preferred_element_type=f32)
    share_up = ffw // n_tok
    for d in range(n_tok):
        nar_s[d] = jnp.concatenate(
            [spread[0:8, d * 128 : (d + 1) * 128]]
            + [bup_v[0:1, d * share_up + i : d * share_up + i + 128] for i in range(0, share_up, 128)]
            + [jnp.zeros((8 - share_up // 128, 128), f32)], axis=0)

    def nar_copy(k):
        return remote(nar_s.at[me ^ k], nar_r.at[k], nt_ss.at[k], nt_rs.at[k], (grp, me ^ k))

    def nar_cross(k):
        return remote(nar_g, nar_h.at[k], ng_ss.at[k], ng_rs.at[k], (grp ^ k, me))

    for k in order:
        nar_copy(k).start()
    step_r1(3)
    step_rb(0)
    step_r2(1)
    step_r2(2)
    total = nar_s[me]
    for k in order:
        nar_copy(k).wait_recv()
        total += nar_r[k]
    nar_g[...] = total
    for k in (3, 1, 2):
        nar_cross(k).start()
    step_r2(3)
    step_ra(1)
    step_ra(2)
    step_ra(3)
    step_rb(1)
    step_rb(2)
    total = nar_g[...]
    for k in (1, 2, 3):
        nar_cross(k).wait_recv()
        total += nar_h[k]
    nar_t[...] = total
    nar_out = pltpu.make_async_copy(nar_t, nar_o, own_sem.at[2])
    nar_out.start()
    step_rb(3)

    own_bo.wait()
    own_gt.wait()
    nar_out.wait()
    for k in order:
        row_copy(back_ref, bo_got, bo_ss, bo_rs, k).wait()
        row_copy(gdown, gt_got, gt_ss, gt_rs, k).wait()
        nar_copy(k).wait_send()
    for k in (1, 2, 3):
        nar_cross(k).wait_send()
    for m in range(4):
        own_ag(m).wait()
        for z in range(chips):
            copy_s0(m, z).wait_send()
            copy_x1(m, z).wait_send()
            copy_x2(m, z).wait_send()
        copy_za(m, 0).wait_send()
        copy_za(m, 1).wait_send()
        copy_zb(m).wait_send()
        for k in (1, 2, 3):
            copy_ag(m, k).wait()


def backward(n_tok, saved, w_qkv, w_out, w_up, w_down, norm1_gain, norm2_gain):
    rows, width = saved[0].shape
    ffw = w_up.shape[1]
    per = rows // n_tok
    chips = n_tok // 2
    kinds = grad_kinds(width, ffw, n_tok)
    vm = pl.BlockSpec(memory_space=pltpu.VMEM)
    hb = pl.BlockSpec(memory_space=pl.ANY)
    outs = [((rows, width), bf16), ((rows, width), bf16), ((16, 128), f32)]
    outs += [(kind, bf16) for kind in kinds]
    vmem = pltpu.VMEM
    dma = pltpu.SemaphoreType.DMA
    scratch = [
        vmem(w_qkv.shape, bf16), vmem(w_out.shape, bf16), vmem(w_up.shape, bf16), vmem(w_down.shape, bf16),
        vmem(w_down.shape, bf16), vmem((rows, ffw), bf16), vmem((rows, ffw), bf16), vmem((rows, width), bf16),
        vmem((rows, width), bf16), vmem((rows, width), f32), vmem((rows, width), f32), vmem((rows, width), bf16),
        vmem((rows, width), bf16), vmem((rows, width), bf16), vmem((rows, 3 * width), bf16),
        vmem((rows * H // 2, 2 * CLU), bf16), vmem(w_down.shape, bf16), vmem((rows, 128), f32),
        vmem((16, width), f32), vmem((8, ffw), f32), vmem((n_tok, 16, 128), f32), vmem((n_tok, 16, 128), f32),
        vmem((16, 128), f32), vmem((4, 16, 128), f32), vmem((16, 128), f32),
        dma((15,)), dma((n_tok,)), dma((n_tok,)), dma((n_tok,)), dma((n_tok,)), dma((3,)),
    ]
    scratch += [dma((4, chips))] * 6 + [dma((4, 2))] * 2 + [dma((4,))] * 2
    scratch += [dma((4, 4))] * 2 + [dma((4,)), pltpu.SemaphoreType.REGULAR((2,))]
    scratch += [dma((n_tok,))] * 2 + [dma((4,))] * 2
    return pl.pallas_call(
        functools.partial(backward_kernel, n_tok, per, kinds),
        out_shape=[jax.ShapeDtypeStruct(s, d) for s, d in outs],
        in_specs=[hb] * 16 + [vm] * 2,
        out_specs=[hb] * len(outs),
        scratch_shapes=scratch,
        compiler_params=pltpu.CompilerParams(
            collective_id=1, has_side_effects=True, vmem_limit_bytes=63 * 2**20
        ),
        name="layer_backward",
    )(*saved, w_qkv, w_out, w_up, w_down, norm1_gain, norm2_gain)[:7]


def finish_kernel(pos_ref, bo_ref, gt_ref, nar_ref, wd_ref, wu_ref, wo_ref, wq_ref, *outs):
    (out_o, tok_o, wq_o, bq_o, bv_o, wo_o, b_out_o, g1_o, s1_o, wu_o, bu_o, wd_o, bd_o, g2_o, s2_o) = outs
    rows = bo_ref.shape[0]
    column = column_of(pos_ref[0:1, :].astype(f32))
    for b in range(rows // BLK):
        sl = pl.ds(b * BLK, BLK)
        home = hot_from_column(column[b * BLK : (b + 1) * BLK], rows)
        out_o[sl, :] = dot32(home, bo_ref[...]).astype(bf16)
        tok_o[sl, :] = dot32(home, gt_ref[...]).astype(bf16)
    for src, dst in ((wd_ref, wd_o), (wu_ref, wu_o), (wo_ref, wo_o), (wq_ref, wq_o)):
        dst[...] = src[...].astype(f32)
    for i, dst in enumerate((bq_o, bv_o, b_out_o, g1_o, s1_o, bd_o, g2_o, s2_o)):
        dst[...] = nar_ref[i, 0 : dst.shape[0]]
    for i in range(bu_o.shape[0] // 128):
        bu_o[i * 128 : (i + 1) * 128] = nar_ref[8 + i, :]


def finish(pos, got):
    bo, gt, nar, wd, wu, wo, wq = got
    rows, width = bo.shape
    each = wq.shape[0]
    vm = pl.BlockSpec(memory_space=pltpu.VMEM)
    outs = [
        (bo.shape, bf16), (gt.shape, bf16), (wq.shape, f32), ((each,), f32), ((each,), f32), (wo.shape, f32),
        ((each,), f32), ((each,), f32), ((each,), f32), (wu.shape, f32), ((wd.shape[0],), f32), (wd.shape, f32),
        ((each,), f32), ((each,), f32), ((each,), f32),
    ]
    return pl.pallas_call(
        finish_kernel,
        out_shape=[jax.ShapeDtypeStruct(s, d) for s, d in outs],
        in_specs=[vm] * 8,
        out_specs=[vm] * len(outs),
        compiler_params=pltpu.CompilerParams(vmem_limit_bytes=60 * 2**20),
        name="back_home",
    )(pos, bo, gt, nar, wd, wu, wo, wq)


def per_device_fast(
    tokens_in, w_qkv, b_query, b_value, w_out, b_out, norm1_gain, norm1_shift,
    w_up, b_up, w_down, b_down, norm2_gain, norm2_shift, out_grad, doc_lengths, cluster_slots,
):
    n_tok = lax.axis_size("tok")
    *saved, pos = forward(
        n_tok, tokens_in, w_qkv, b_query, b_value, w_out, b_out, norm1_gain, norm1_shift,
        w_up, b_up, w_down, b_down, norm2_gain, norm2_shift, out_grad, doc_lengths, cluster_slots)
    got = backward(n_tok, saved, w_qkv, w_out, w_up, w_down, norm1_gain, norm2_gain)
    return tuple(finish(pos, got))


def norm_rows(values, scales, shifts):
    centre = values - jnp.mean(values, axis=-1, keepdims=True)
    spread = jnp.mean(centre * centre, axis=-1, keepdims=True)
    return centre * lax.rsqrt(spread + eps) * scales + shifts


def gelu_exact(values):
    return jax.nn.gelu(values, approximate=False)


def valid_tokens(lengths_row, offset, amount, cluster):
    padded = (lengths_row + cluster - 1) // cluster * cluster
    starts = jnp.cumsum(padded) - padded
    position = offset + jnp.arange(amount, dtype=jnp.int32)
    inside = (position[:, None] >= starts[None, :]) & (
        position[:, None] < (starts + lengths_row)[None, :]
    )
    return jnp.any(inside, axis=1)


def move(one_hot, rows):
    return dot32(one_hot, rows).astype(jnp.bfloat16)


def move_back(one_hot, rows):
    picked = jnp.einsum("pi,pd->id", one_hot, rows, preferred_element_type=jnp.float32)
    return picked.astype(jnp.bfloat16)


def exchange(rows):
    return lax.all_to_all(rows, "tok", split_axis=0, concat_axis=0, tiled=True)


def per_device(
    tokens_in, w_qkv, b_query, b_value, w_out, b_out, norm1_gain, norm1_shift,
    w_up, b_up, w_down, b_down, norm2_gain, norm2_shift, out_grad, doc_lengths, cluster_slots,
):
    tok_dev, width = tokens_in.shape
    head_size = width // H
    clusters = tok_dev // CLU
    n_tok = lax.axis_size("tok")
    per_peer = tok_dev // n_tok
    my_index = lax.axis_index("tok")
    f32 = jnp.float32

    usable = valid_tokens(doc_lengths[0], my_index * tok_dev, tok_dev, CLU)
    dest = cluster_slots // tok_dev
    dest_hot = (dest[:, None] == jnp.arange(n_tok)[None, :]).astype(jnp.int32)
    rank = jnp.sum((jnp.cumsum(dest_hot, axis=0) - dest_hot) * dest_hot, axis=1)
    send_pos = dest * per_peer + rank
    send_hot = (jnp.arange(tok_dev)[:, None] == send_pos[None, :])
    note = (cluster_slots % tok_dev) * 2 + usable.astype(jnp.int32)
    sent_note = jnp.sum(jnp.where(send_hot, note[None, :], 0), axis=1)
    send_hot = send_hot.astype(jnp.bfloat16)
    got_note = exchange(sent_note)
    x_got = exchange(move(send_hot, tokens_in))
    g_got = exchange(move(send_hot, out_grad))
    place_hot = jnp.arange(tok_dev)[:, None] == (got_note // 2)[None, :]
    key_live = jnp.sum(jnp.where(place_hot, got_note[None, :] % 2, 0), axis=1) > 0
    place_hot = place_hot.astype(jnp.bfloat16)
    x = move(place_hot, x_got)

    bias_qkv = jnp.concatenate(
        [b_query.astype(f32), jnp.zeros((width,), f32), b_value.astype(f32)]
    )
    qkv = (dot32(x, w_qkv) + bias_qkv).astype(jnp.bfloat16)
    packed = qkv.reshape(clusters, CLU, 3, H, head_size)
    query, keys, value = packed[:, :, 0], packed[:, :, 1], packed[:, :, 2]
    scale = head_size ** (-0.5)
    scores = jnp.einsum("bqhd,bkhd->bhqk", query, keys, preferred_element_type=f32) * scale
    scores = jnp.where(key_live.reshape(clusters, 1, 1, CLU), scores, masked_score)
    expo = jnp.exp(scores - jnp.max(scores, axis=-1, keepdims=True))
    probs = expo / jnp.sum(expo, axis=-1, keepdims=True)
    weights = probs.astype(jnp.bfloat16)
    context = jnp.einsum("bhqk,bkhd->bqhd", weights, value, preferred_element_type=f32)
    context = context.astype(jnp.bfloat16).reshape(tok_dev, width)

    resid1 = x.astype(f32) + dot32(context, w_out) + b_out.astype(f32)
    normed1, norm1_back = jax.vjp(
        norm_rows, resid1, norm1_gain.astype(f32), norm1_shift.astype(f32)
    )
    normed1_low = normed1.astype(jnp.bfloat16)
    up_pre = dot32(normed1_low, w_up) + b_up.astype(f32)
    gelu_out, gelu_back = jax.vjp(gelu_exact, up_pre)
    gelu_low = gelu_out.astype(jnp.bfloat16)
    down_out = dot32(gelu_low, w_down) + b_down.astype(f32)
    normed2, norm2_back = jax.vjp(
        norm_rows, normed1 + down_out, norm2_gain.astype(f32), norm2_shift.astype(f32)
    )
    out_got = exchange(move_back(place_hot, normed2.astype(jnp.bfloat16)))
    block_out = move_back(send_hot, out_got)

    g = move(place_hot, g_got)
    grad_resid2, grad_gain2, grad_shift2 = norm2_back(g.astype(f32))
    grad_down = grad_resid2.astype(jnp.bfloat16)
    grad_b_down = jnp.sum(grad_down.astype(f32), axis=0)
    grad_w_down = jnp.einsum("nf,nd->fd", gelu_low, grad_down, preferred_element_type=f32)
    grad_gelu = jnp.einsum("nd,fd->nf", grad_down, w_down, preferred_element_type=f32)
    grad_up = gelu_back(grad_gelu)[0].astype(jnp.bfloat16)
    grad_b_up = jnp.sum(grad_up.astype(f32), axis=0)
    grad_w_up = jnp.einsum("nd,nf->df", normed1_low, grad_up, preferred_element_type=f32)
    grad_normed1 = grad_resid2 + jnp.einsum(
        "nf,df->nd", grad_up, w_up, preferred_element_type=f32
    )
    grad_resid1, grad_gain1, grad_shift1 = norm1_back(grad_normed1)
    grad_attn = grad_resid1.astype(jnp.bfloat16)
    grad_b_out = jnp.sum(grad_attn.astype(f32), axis=0)
    grad_w_out = jnp.einsum("nd,ne->de", context, grad_attn, preferred_element_type=f32)
    grad_context = jnp.einsum("ne,de->nd", grad_attn, w_out, preferred_element_type=f32)
    grad_context = grad_context.astype(jnp.bfloat16).reshape(clusters, CLU, H, head_size)

    grad_probs = jnp.einsum("bqhd,bkhd->bhqk", grad_context, value, preferred_element_type=f32)
    row_dot = jnp.sum(grad_probs * probs, axis=-1, keepdims=True)
    grad_scores = (probs * (grad_probs - row_dot)).astype(jnp.bfloat16)
    grad_q = jnp.einsum("bhqk,bkhd->bqhd", grad_scores, keys, preferred_element_type=f32) * scale
    grad_k = jnp.einsum("bhqk,bqhd->bkhd", grad_scores, query, preferred_element_type=f32) * scale
    grad_v = jnp.einsum("bhqk,bqhd->bkhd", weights, grad_context, preferred_element_type=f32)
    grad_qkv = jnp.stack([grad_q, grad_k, grad_v], axis=2).astype(jnp.bfloat16)
    grad_qkv = grad_qkv.reshape(tok_dev, 3 * width)
    grad_total = grad_resid1 + jnp.einsum(
        "ne,de->nd", grad_qkv, w_qkv, preferred_element_type=f32
    )
    back_got = exchange(move_back(place_hot, grad_total.astype(jnp.bfloat16)))
    grad_tokens = move_back(send_hot, back_got)
    grad_w_qkv = jnp.einsum("nd,ne->de", x, grad_qkv, preferred_element_type=f32)
    grad_qkv_sum = jnp.sum(grad_qkv.astype(f32), axis=0)

    low = jnp.bfloat16
    wide = jnp.concatenate(
        [
            grad_w_qkv.astype(low), grad_w_out.astype(low), grad_w_up.astype(low),
            grad_w_down.astype(low).reshape(width, -1),
        ],
        axis=1,
    )
    narrow = jnp.concatenate(
        [
            member.reshape(n_tok, -1)
            for member in (
                grad_qkv_sum[:width], grad_qkv_sum[2 * width :], grad_b_out, grad_gain1,
                grad_shift1, grad_b_down, grad_gain2, grad_shift2, grad_b_up,
            )
        ],
        axis=1,
    )
    share = lax.psum_scatter(wide, "tok", scatter_dimension=0, tiled=True)
    share = lax.psum(share, "grp").astype(f32)
    narrow = lax.psum(narrow, ("grp", "tok"))
    mine = lax.dynamic_index_in_dim(narrow, my_index, 0, keepdims=False)
    step = width // n_tok
    parts = [mine[i * step : (i + 1) * step] for i in range(8)] + [mine[8 * step :]]
    ffw = w_up.shape[1]
    return (
        block_out,
        grad_tokens,
        share[:, : 3 * width],
        parts[0],
        parts[1],
        share[:, 3 * width : 4 * width],
        parts[2],
        parts[3],
        parts[4],
        share[:, 4 * width : 4 * width + ffw],
        parts[8],
        share[:, 4 * width + ffw :].reshape(ffw // n_tok, width),
        parts[5],
        parts[6],
        parts[7],
    )


def solution(mesh):
    n_tok = mesh.shape["tok"]

    def body(*args):
        fits = n_tok == 8 and mesh.shape["grp"] == 4 and args[0].shape[0] == 1024
        return (per_device_fast if fits else per_device)(*args)

    rows = P(("grp", "tok"), None)
    in_specs = (rows,) + (P(),) * 13 + (rows, P("grp", None), P(("grp", "tok")))
    shares = (
        P("tok", None), P("tok"), P("tok"), P("tok", None), P("tok"), P("tok"), P("tok"),
        P("tok", None), P("tok"), P("tok", None), P("tok"), P("tok"), P("tok"),
    )
    return jax.shard_map(
        body, mesh=mesh, in_specs=in_specs, out_specs=(rows, rows) + shares, check_vma=False
    )
```

profile of v0, /device:TPU:0, one launch (start us, length us, event | category | flops | bytes accessed | tf_op | source)
XLA Modules:
  0.0 226.2 jit_solution(5666569584877554571)
XLA Ops:
  0.6 81.6 %layer_forward.1 = (bf16[1024,768]{1,0:T(8,128)(2,1)}, bf16[1024,768]{1,0:T(8,128)(2,1)}, bf16[1024,2304]{1,0:T(8,128)(2,1)}, bf16[6144,256]{1,0:T(8,128)(2,1)},...) custom-call(s32[1024]{0:T(1024)} %slots_ref.1, ...), custom_call_target="tpu_custom_call" | custom-call | tf_op jit(solution)/shard_map/layer_forward/pallas_call | solution.py:351
  82.2 135.1 %layer_backward.1 = (bf16[1024,768]{1,0:T(8,128)(2,1)}, bf16[1024,768]{1,0:T(8,128)(2,1)}, f32[16,128]{1,0:T(8,128)}, bf16[384,768]{1,0:T(8,128)(2,1)}, bf16[96,...) custom-call(bf16[1024,768]{1,0:T(8,128)(2,1)} %get-tuple-element.36.refs_0_, ...), custom_call_target="tpu_custom_call" | custom-call | tf_op jit(solution)/shard_map/layer_backward/pallas_call | solution.py:809
  217.4 8.6 %back_home.1 = (bf16[1024,768]{1,0:T(8,128)(2,1)}, bf16[1024,768]{1,0:T(8,128)(2,1)}, f32[96,2304]{1,0:T(8,128)}, f32[96]{0:T(128)}, f32[96]{0:T(128)}, /*index=...) custom-call(s32[8,1024]{1,0:T(8,128)} %get-tuple-element.35.pos_ref,, ...), custom_call_target="tpu_custom_call" | custom-call | tf_op jit(solution)/shard_map/back_home/pallas_call | solution.py:849
where the time goes:
time: 229 us; the launch traced here: 226 us
  Pallas kernels  225 us (98%)
    pallas_call x1, Pallas kernels, backward(): pl.pallas_call(functools.partial(backward_kernel, n_tok, per, kinds), out...  135 us
    pallas_call x1, Pallas kernels, forward(): pl.pallas_call(functools.partial(forward_kernel, n_tok, per), out_shape=[...  81.6 us
    pallas_call x1, Pallas kernels, finish(): pl.pallas_call(finish_kernel, out_shape=[jax.ShapeDtypeStruct(s, d) for s...  8.64 us

commit v1 on v0

--- a/solution.py
+++ b/solution.py
@@ -46,10 +46,10 @@
     return centre * rstd, rstd
 
 
-def lane_halves(width):
+def lane_halves(width, factor=1.0):
     lane = lax.broadcasted_iota(jnp.int32, (1, width), 1)
-    low = (lane < width // 2).astype(f32)
-    return low.astype(bf16), (1.0 - low).astype(bf16)
+    low = (lane < width // 2).astype(f32) * factor
+    return low.astype(bf16), (factor - low).astype(bf16)
 
 
 def stack_heads(pair, halves):
@@ -221,8 +221,9 @@
         copy.wait()
 
     halves = lane_halves(2 * width // H)
+    scaled = lane_halves(2 * width // H, (width // H) ** (-0.5))
     pair_width = 2 * width // H
-    scale = (width // H) ** (-0.5)
+    pairs = range(H // 2)
     outs = (
         (qkv_t, qkv_o, BLK), (p_t, p_o, BLK * H // 2), (ctx_t, ctx_o, BLK), (r1_t, r1_o, BLK),
         (n1_t, n1_o, BLK), (gelu_t, gelu_o, BLK), (gelup_t, gelup_o, BLK), (r2_t, r2_o, BLK),
@@ -254,17 +255,16 @@
             live = live_s[pl.ds(at, CLU), :] > 0.5
             live = jnp.concatenate([live, live], axis=1)
             crow = pl.ds(c * CLU, CLU)
-            for p in range(H // 2):
-                cols = [pl.ds(part * width + p * pair_width, pair_width) for part in range(3)]
-                q2 = stack_heads(qkv_t[slot, crow, cols[0]], halves)
-                k2 = qkv_t[slot, crow, cols[1]]
-                v2 = stack_heads(qkv_t[slot, crow, cols[2]], halves)
-                scores = jnp.where(live, dot_rows(k2, q2) * scale, masked_score)
-                expo = jnp.exp(scores - jnp.max(scores, axis=0, keepdims=True))
-                weights = (expo / jnp.sum(expo, axis=0, keepdims=True)).astype(bf16)
-                p_t[slot, pl.ds((c * (H // 2) + p) * CLU, CLU), :] = weights
-                context = dot_cols(one_over_other(weights), v2)
-                ctx_t[slot, crow, pl.ds(p * pair_width, pair_width)] = context.astype(bf16)
+            cols = [[pl.ds(part * width + p * pair_width, pair_width) for p in pairs] for part in range(3)]
+            q2 = [stack_heads(qkv_t[slot, crow, cols[0][p]], scaled) for p in pairs]
+            scores = [jnp.where(live, dot_rows(qkv_t[slot, crow, cols[1][p]], q2[p]), masked_score) for p in pairs]
+            expo = [jnp.exp(member - jnp.max(member, axis=0, keepdims=True)) for member in scores]
+            weights = [(member / jnp.sum(member, axis=0, keepdims=True)).astype(bf16) for member in expo]
+            v2 = [stack_heads(qkv_t[slot, crow, cols[2][p]], halves) for p in pairs]
+            context = [dot_cols(one_over_other(weights[p]), v2[p]).astype(bf16) for p in pairs]
+            for p in pairs:
+                p_t[slot, pl.ds((c * (H // 2) + p) * CLU, CLU), :] = weights[p]
+                ctx_t[slot, crow, cols[0][p]] = context[p]
         resid1 = x.astype(f32) + (dot32(ctx_t[slot], wo[...]) + row_of(bo_ref))
         r1_t[slot] = resid1
         hat1, _ = norm_parts(resid1)
@@ -534,28 +534,30 @@
     def add_in(target, extra):
         target[...] = target[...] + extra[...]
 
+    turns = (0, 2, 1, 3)
+
     def start_s0(m):
-        for z in range(chips):
+        for z in turns:
             copy_s0(m, z).start()
 
-    def step_r0(m, zs=None):
+    def step_r0(m, zs=turns):
         share, cols = kinds[m]
-        for z in zs or range(chips):
+        for z in zs:
             copy_s0(m, z).wait_recv()
             add_in(held(m, z, 0, share, 0, cols), land_s0(m, z))
             copy_x1(m, z).start()
 
-    def step_r1(m):
+    def step_r1(m, zs=turns):
         share, cols = kinds[m]
         half, hcols = share // 2, cols // 2
-        for z in range(chips):
+        for z in zs:
             copy_x1(m, z).wait_recv()
             spot = (0, share, gx * hcols, hcols) if first_x(z) else (gy * half, half, 0, cols)
             add_in(held(m, z, *spot), land_x1(m, z))
             copy_x2(m, z).start()
 
     def step_r2(m):
-        for z in range(chips):
+        for z in turns:
             copy_x2(m, z).wait_recv()
             add_in(quarter(m, z), land_x2(m, z))
         copy_za(m, 0).start()
@@ -611,15 +613,13 @@
     ready("gelu")
     begin("wu", "r1", "wo", "n1", "ctx")
     step = width
-    for j in range(ffw // step):
+    for j in turns:
         cs = pl.ds(j * step, step)
         gwd[cs, :] = dot_cols(gelu[:, cs], gdown[...]).astype(bf16)
-        if step == 2 * kinds[0][0]:
-            copy_s0(0, j).start()
-    if step != 2 * kinds[0][0]:
-        start_s0(0)
+        copy_s0(0, j).start()
     tell_free(0)
     ready("wd", "gelup")
+    step_r0(0, turns[:2])
     for b in range(blocks):
         sl = pl.ds(b * BLK, BLK)
         for j in range(ffw // step):
@@ -628,13 +628,26 @@
             gup[sl, cs] = up
             bup_v[0:1, cs] += jnp.sum(up.astype(f32), axis=0, keepdims=True)
         if b == 1:
-            step_r0(0, (0, 1))
-    step_r0(0, (2, 3))
+            step_r0(0, turns[2:])
     begin("qkv", "p", "wq", "col")
-    ready("wu", "r1", "wo")
+    ready("wu", "n1")
     for b in range(blocks):
         sl = pl.ds(b * BLK, BLK)
-        gn1 = grow[sl, :] + dot_rows(gup[sl, :], wu[...])
+        grow[sl, :] += dot_rows(gup[sl, :], wu[...])
+    for j in range(ffw // step):
+        cs = pl.ds(j * step, step)
+        wu[:, cs] = dot_cols(low1[...], gup[:, cs]).astype(bf16)
+        if j == 0:
+            step_r1(0, turns[:2])
+        elif j == 2:
+            step_r1(0, turns[2:])
+    tell_free(1)
+    partners_free(0)
+    start_s0(1)
+    ready("r1", "wo", "ctx")
+    for b in range(blocks):
+        sl = pl.ds(b * BLK, BLK)
+        gn1 = grow[sl, :]
         back, hat = norm_back(gn1, resid[sl, :], gain1)
         low = back.astype(bf16)
         grow[sl, :] = back
@@ -643,45 +656,41 @@
         add_sum(3, gn1 * hat)
         add_sum(4, gn1)
         gcl[sl, :] = dot_rows(low, wo[...]).astype(bf16)
-    ready("n1")
-    for j in range(ffw // step):
-        cs = pl.ds(j * step, step)
-        wu[:, cs] = dot_cols(low1[...], gup[:, cs]).astype(bf16)
-    tell_free(1)
-    partners_free(0)
-    start_s0(1)
-    ready("ctx")
+        if b == 2:
+            step_r0(1, turns[:2])
     wo[...] = dot_cols(ctx[...], gattn[...]).astype(bf16)
     begin("xc")
     partners_free(1)
     start_s0(2)
-    step_r1(0)
+    step_r0(1, turns[2:])
+    step_r2(0)
 
     ready("qkv", "p", "wq")
     halves = lane_halves(2 * width // H)
     pair_width = 2 * width // H
-    scale = (width // H) ** (-0.5)
+    scaled = lane_halves(2 * width // H, (width // H) ** (-0.5))
+    pairs = range(H // 2)
 
     def attend(b):
         for c in range(BLK // CLU):
             crow = pl.ds(b * BLK + c * CLU, CLU)
-            for p in range(H // 2):
-                cols = [pl.ds(part * width + p * pair_width, pair_width) for part in range(3)]
-                q2 = stack_heads(qkv[crow, cols[0]], halves)
-                k2 = stack_heads(qkv[crow, cols[1]], halves)
-                v2 = qkv[crow, cols[2]]
-                go = stack_heads(gcl[crow, pl.ds(p * pair_width, pair_width)], halves)
-                weights = probs[pl.ds(((b * BLK // CLU + c) * (H // 2) + p) * CLU, CLU), :]
-                weights32 = weights.astype(f32)
-                gp = dot_rows(v2, go)
-                dot = jnp.sum(gp * weights32, axis=0, keepdims=True)
-                gs = (weights32 * (gp - dot)).astype(bf16)
-                gq = (dot_cols(one_over_other(gs), k2) * scale).astype(bf16)
-                gk = (dot32(gs, q2) * scale).astype(bf16)
-                gv = dot32(weights, go).astype(bf16)
-                qkv[crow, cols[0]] = gq
-                qkv[crow, cols[1]] = gk
-                qkv[crow, cols[2]] = gv
+            cols = [[pl.ds(part * width + p * pair_width, pair_width) for p in pairs] for part in range(3)]
+            first = (b * BLK // CLU + c) * (H // 2)
+            go = [stack_heads(gcl[crow, cols[0][p]], halves) for p in pairs]
+            gp = [dot_rows(qkv[crow, cols[2][p]], go[p]) for p in pairs]
+            weights = [probs[pl.ds((first + p) * CLU, CLU), :] for p in pairs]
+            gv = [dot32(weights[p], go[p]).astype(bf16) for p in pairs]
+            wide = [member.astype(f32) for member in weights]
+            dots = [jnp.sum(gp[p] * wide[p], axis=0, keepdims=True) for p in pairs]
+            gs = [(wide[p] * (gp[p] - dots[p])).astype(bf16) for p in pairs]
+            q2 = [stack_heads(qkv[crow, cols[0][p]], scaled) for p in pairs]
+            k2 = [stack_heads(qkv[crow, cols[1][p]], scaled) for p in pairs]
+            gk = [dot32(gs[p], q2[p]).astype(bf16) for p in pairs]
+            gq = [dot_cols(one_over_other(gs[p]), k2[p]).astype(bf16) for p in pairs]
+            for p in pairs:
+                qkv[crow, cols[0][p]] = gq[p]
+                qkv[crow, cols[1][p]] = gk[p]
+                qkv[crow, cols[2][p]] = gv[p]
         sl = pl.ds(b * BLK, BLK)
         add_sum(0, qkv[sl, 0:width].astype(f32))
         add_sum(1, qkv[sl, 2 * width :].astype(f32))
@@ -689,27 +698,29 @@
         low1[sl, :] = total.astype(bf16)
 
     attend(0)
+    step_r0(2)
     attend(1)
-    step_r0(1)
-    step_r0(2)
+    step_ra(0)
     attend(2)
-    step_r2(0)
+    step_r1(1, turns[:2])
     attend(3)
+    step_r1(1, turns[2:])
     ready("xc", "col")
+    for b in range(blocks):
+        sl = pl.ds(b * BLK, BLK)
+        gdown[sl, :] = dot32(hot_from_column(col[sl, :], rows), low1[...]).astype(bf16)
+    def send_home(*who):
+        for k in who:
+            row_copy(gdown, gt_got, gt_ss, gt_rs, k).start()
+
+    send_home(7, 6, 1)
+    own_gt = pltpu.make_async_copy(gdown.at[mine], gt_got.at[mine], own_sem.at[1])
+    own_gt.start()
+    step_rb(0)
     for j in range(3):
         cs = pl.ds(j * step, step)
         wq[:, cs] = dot_cols(gattn[...], qkv[:, cs]).astype(bf16)
     start_s0(3)
-    for b in range(blocks):
-        sl = pl.ds(b * BLK, BLK)
-        gdown[sl, :] = dot32(hot_from_column(col[sl, :], rows), low1[...]).astype(bf16)
-    for k in order:
-        row_copy(gdown, gt_got, gt_ss, gt_rs, k).start()
-    own_gt = pltpu.make_async_copy(gdown.at[mine], gt_got.at[mine], own_sem.at[1])
-    own_gt.start()
-    step_ra(0)
-    step_r0(3)
-    step_r1(1)
     step_r1(2)
 
     each = width // n_tok
@@ -733,10 +744,16 @@
 
     for k in order:
         nar_copy(k).start()
-    step_r1(3)
-    step_rb(0)
     step_r2(1)
+    step_r0(3)
     step_r2(2)
+    step_r1(3, turns[:2])
+    step_ra(1)
+    step_ra(2)
+    send_home(5, 4, 3, 2)
+    step_r1(3, turns[2:])
+    step_rb(1)
+    step_rb(2)
     total = nar_s[me]
     for k in order:
         nar_copy(k).wait_recv()
@@ -745,11 +762,6 @@
     for k in (3, 1, 2):
         nar_cross(k).start()
     step_r2(3)
-    step_ra(1)
-    step_ra(2)
-    step_ra(3)
-    step_rb(1)
-    step_rb(2)
     total = nar_g[...]
     for k in (1, 2, 3):
         nar_cross(k).wait_recv()
@@ -757,6 +769,7 @@
     nar_t[...] = total
     nar_out = pltpu.make_async_copy(nar_t, nar_o, own_sem.at[2])
     nar_out.start()
+    step_ra(3)
     step_rb(3)
 
     own_bo.wait()
@@ -819,21 +832,42 @@
     )(*saved, w_qkv, w_out, w_up, w_down, norm1_gain, norm2_gain)[:7]
 
 
-def finish_kernel(pos_ref, bo_ref, gt_ref, nar_ref, wd_ref, wu_ref, wo_ref, wq_ref, *outs):
-    (out_o, tok_o, wq_o, bq_o, bv_o, wo_o, b_out_o, g1_o, s1_o, wu_o, bu_o, wd_o, bd_o, g2_o, s2_o) = outs
-    rows = bo_ref.shape[0]
+def finish_kernel(
+    pos_ref, nar_ref, bo_ref, gt_ref, wd_ref, wu_ref, wo_ref, wq_ref,
+    out_o, tok_o, wq_o, wo_o, wu_o, wd_o, bq_o, bv_o, b_out_o, g1_o, s1_o, bu_o, bd_o, g2_o, s2_o,
+    bo, gt, wd, wu, wo, wq, out_t, tok_t, wd_t, wu_t, wo_t, wq_t, in_sem, out_sem, row_sem,
+):
+    rows = bo.shape[0]
+    ins = [
+        pltpu.make_async_copy(src, dst, in_sem.at[i])
+        for i, (src, dst) in enumerate(
+            ((wd_ref, wd), (wu_ref, wu), (wq_ref, wq), (wo_ref, wo), (bo_ref, bo), (gt_ref, gt))
+        )
+    ]
+    for copy in ins:
+        copy.start()
+    outs = []
+    for i, (src, dst, whole) in enumerate(((wd, wd_t, wd_o), (wu, wu_t, wu_o), (wq, wq_t, wq_o), (wo, wo_t, wo_o))):
+        ins[i].wait()
+        dst[...] = src[...].astype(f32)
+        outs.append(pltpu.make_async_copy(dst, whole, out_sem.at[i]))
+        outs[-1].start()
     column = column_of(pos_ref[0:1, :].astype(f32))
+    ins[4].wait()
+    ins[5].wait()
     for b in range(rows // BLK):
         sl = pl.ds(b * BLK, BLK)
         home = hot_from_column(column[b * BLK : (b + 1) * BLK], rows)
-        out_o[sl, :] = dot32(home, bo_ref[...]).astype(bf16)
-        tok_o[sl, :] = dot32(home, gt_ref[...]).astype(bf16)
-    for src, dst in ((wd_ref, wd_o), (wu_ref, wu_o), (wo_ref, wo_o), (wq_ref, wq_o)):
-        dst[...] = src[...].astype(f32)
+        for i, (got, tile, whole) in enumerate(((bo, out_t, out_o), (gt, tok_t, tok_o))):
+            tile[sl, :] = dot32(home, got[...]).astype(bf16)
+            outs.append(pltpu.make_async_copy(tile.at[sl], whole.at[sl], row_sem.at[i, b]))
+            outs[-1].start()
     for i, dst in enumerate((bq_o, bv_o, b_out_o, g1_o, s1_o, bd_o, g2_o, s2_o)):
         dst[...] = nar_ref[i, 0 : dst.shape[0]]
     for i in range(bu_o.shape[0] // 128):
         bu_o[i * 128 : (i + 1) * 128] = nar_ref[8 + i, :]
+    for copy in outs:
+        copy.wait()
 
 
 def finish(pos, got):
@@ -841,19 +875,23 @@
     rows, width = bo.shape
     each = wq.shape[0]
     vm = pl.BlockSpec(memory_space=pltpu.VMEM)
-    outs = [
-        (bo.shape, bf16), (gt.shape, bf16), (wq.shape, f32), ((each,), f32), ((each,), f32), (wo.shape, f32),
-        ((each,), f32), ((each,), f32), ((each,), f32), (wu.shape, f32), ((wd.shape[0],), f32), (wd.shape, f32),
-        ((each,), f32), ((each,), f32), ((each,), f32),
-    ]
-    return pl.pallas_call(
+    hb = pl.BlockSpec(memory_space=pl.ANY)
+    outs = [(bo.shape, bf16), (gt.shape, bf16), (wq.shape, f32), (wo.shape, f32), (wu.shape, f32), (wd.shape, f32)]
+    outs += [((each,), f32)] * 5 + [((wd.shape[0],), f32)] + [((each,), f32)] * 3
+    vmem = pltpu.VMEM
+    scratch = [vmem(member.shape, bf16) for member in (bo, gt, wd, wu, wo, wq, bo, gt)]
+    scratch += [vmem(member.shape, f32) for member in (wd, wu, wo, wq)]
+    scratch += [pltpu.SemaphoreType.DMA((6,)), pltpu.SemaphoreType.DMA((4,)), pltpu.SemaphoreType.DMA((2, rows // BLK))]
+    (out, tok, g_wq, g_wo, g_wu, g_wd, bq, bv, b_out, g1, s1, bu, bd, g2, s2) = pl.pallas_call(
         finish_kernel,
         out_shape=[jax.ShapeDtypeStruct(s, d) for s, d in outs],
-        in_specs=[vm] * 8,
-        out_specs=[vm] * len(outs),
+        in_specs=[vm] * 2 + [hb] * 6,
+        out_specs=[hb] * 6 + [vm] * 9,
+        scratch_shapes=scratch,
         compiler_params=pltpu.CompilerParams(vmem_limit_bytes=60 * 2**20),
         name="back_home",
-    )(pos, bo, gt, nar, wd, wu, wo, wq)
+    )(pos, nar, bo, gt, wd, wu, wo, wq)
+    return out, tok, g_wq, bq, bv, g_wo, b_out, g1, s1, g_wu, bu, g_wd, bd, g2, s2
 
 
 def per_device_fast(

time: 229 us -> 208 us (0.908)
  Pallas kernels: 225 us -> 204 us
    pallas_call x1, Pallas kernels: 135 us -> 114 us  [backward(): pl.pallas_call(functools.partial(backward_kernel, n_tok, per, kinds), out...]
where the time goes in v1:
time: 208 us; the launch traced here: 205 us
  Pallas kernels  204 us (98%)
    pallas_call x1, Pallas kernels, backward(): pl.pallas_call(functools.partial(backward_kernel, n_tok, per, kinds), out...  114 us
    pallas_call x1, Pallas kernels, forward(): pl.pallas_call(functools.partial(forward_kernel, n_tok, per), out_shape=[...  81.6 us
    pallas_call x1, Pallas kernels, finish(): pl.pallas_call(finish_kernel, out_shape=[jax.ShapeDtypeStruct(s, d) for s...  8.91 us

profile of v1, /device:TPU:0, one launch (start us, length us, event | category | flops | bytes accessed | tf_op | source)
XLA Modules:
  0.0 205.3 jit_solution(2191874310637066914)
XLA Ops:
  0.6 81.6 %layer_forward.1 = (bf16[1024,768]{1,0:T(8,128)(2,1)}, bf16[1024,768]{1,0:T(8,128)(2,1)}, bf16[1024,2304]{1,0:T(8,128)(2,1)}, bf16[6144,256]{1,0:T(8,128)(2,1)},...) custom-call(s32[1024]{0:T(1024)} %slots_ref.1, ...), custom_call_target="tpu_custom_call" | custom-call | tf_op jit(solution)/shard_map/layer_forward/pallas_call | solution.py:351
  82.2 113.9 %layer_backward.1 = (bf16[1024,768]{1,0:T(8,128)(2,1)}, bf16[1024,768]{1,0:T(8,128)(2,1)}, f32[16,128]{1,0:T(8,128)}, bf16[384,768]{1,0:T(8,128)(2,1)}, bf16[96,...) custom-call(bf16[1024,768]{1,0:T(8,128)(2,1)} %get-tuple-element.51.refs_0_, ...), custom_call_target="tpu_custom_call" | custom-call | tf_op jit(solution)/shard_map/layer_backward/pallas_call | solution.py:822
  196.1 8.9 %back_home.1 = (bf16[1024,768]{1,0:T(8,128)(2,1)}, bf16[1024,768]{1,0:T(8,128)(2,1)}, f32[96,2304]{1,0:T(8,128)}, f32[96,768]{1,0:T(8,128)}, f32[96,3072]{1,0:T(...) custom-call(s32[8,1024]{1,0:T(8,128)} %get-tuple-element.50.pos_ref,, ...), custom_call_target="tpu_custom_call" | custom-call | tf_op jit(solution)/shard_map/back_home/pallas_call | solution.py:885

commit v2 on v1

--- a/solution.py
+++ b/solution.py
@@ -750,7 +750,7 @@
     step_r1(3, turns[:2])
     step_ra(1)
     step_ra(2)
-    send_home(5, 4, 3, 2)
+    send_home(5, 3, 2)
     step_r1(3, turns[2:])
     step_rb(1)
     step_rb(2)
@@ -770,6 +770,7 @@
     nar_out = pltpu.make_async_copy(nar_t, nar_o, own_sem.at[2])
     nar_out.start()
     step_ra(3)
+    send_home(4,)
     step_rb(3)
 
     own_bo.wait()
@@ -841,27 +842,35 @@
     ins = [
         pltpu.make_async_copy(src, dst, in_sem.at[i])
         for i, (src, dst) in enumerate(
-            ((wd_ref, wd), (wu_ref, wu), (wq_ref, wq), (wo_ref, wo), (bo_ref, bo), (gt_ref, gt))
+            ((bo_ref, bo), (gt_ref, gt), (wd_ref, wd), (wu_ref, wu), (wq_ref, wq), (wo_ref, wo))
         )
     ]
     for copy in ins:
         copy.start()
     outs = []
-    for i, (src, dst, whole) in enumerate(((wd, wd_t, wd_o), (wu, wu_t, wu_o), (wq, wq_t, wq_o), (wo, wo_t, wo_o))):
+    column = column_of(pos_ref[0:1, :].astype(f32))
+    home = [hot_from_column(column[b * BLK : (b + 1) * BLK], rows) for b in range(rows // BLK)]
+
+    def widen(i, src, dst, whole):
         ins[i].wait()
         dst[...] = src[...].astype(f32)
-        outs.append(pltpu.make_async_copy(dst, whole, out_sem.at[i]))
+        outs.append(pltpu.make_async_copy(dst, whole, out_sem.at[i - 2]))
         outs[-1].start()
-    column = column_of(pos_ref[0:1, :].astype(f32))
-    ins[4].wait()
-    ins[5].wait()
-    for b in range(rows // BLK):
-        sl = pl.ds(b * BLK, BLK)
-        home = hot_from_column(column[b * BLK : (b + 1) * BLK], rows)
-        for i, (got, tile, whole) in enumerate(((bo, out_t, out_o), (gt, tok_t, tok_o))):
-            tile[sl, :] = dot32(home, got[...]).astype(bf16)
+
+    def bring(i, got, tile, whole):
+        ins[i].wait()
+        for b in range(rows // BLK):
+            sl = pl.ds(b * BLK, BLK)
+            tile[sl, :] = dot32(home[b], got[...]).astype(bf16)
             outs.append(pltpu.make_async_copy(tile.at[sl], whole.at[sl], row_sem.at[i, b]))
             outs[-1].start()
+
+    bring(0, bo, out_t, out_o)
+    widen(2, wd, wd_t, wd_o)
+    widen(3, wu, wu_t, wu_o)
+    widen(4, wq, wq_t, wq_o)
+    widen(5, wo, wo_t, wo_o)
+    bring(1, gt, tok_t, tok_o)
     for i, dst in enumerate((bq_o, bv_o, b_out_o, g1_o, s1_o, bd_o, g2_o, s2_o)):
         dst[...] = nar_ref[i, 0 : dst.shape[0]]
     for i in range(bu_o.shape[0] // 128):

time: 208 us -> 207 us (level)
  no operation moved by 1% of the time
where the time goes in v2:
time: 207 us; the launch traced here: 204 us
  Pallas kernels  203 us (98%)
    pallas_call x1, Pallas kernels, backward(): pl.pallas_call(functools.partial(backward_kernel, n_tok, per, kinds), out...  114 us
    pallas_call x1, Pallas kernels, forward(): pl.pallas_call(functools.partial(forward_kernel, n_tok, per), out_shape=[...  81.6 us
    pallas_call x1, Pallas kernels, finish(): pl.pallas_call(finish_kernel, out_shape=[jax.ShapeDtypeStruct(s, d) for s...  7.52 us

profile of v2, /device:TPU:0, one launch (start us, length us, event | category | flops | bytes accessed | tf_op | source)
XLA Modules:
  0.0 204.0 jit_solution(7896443713517015187)
XLA Ops:
  0.6 81.6 %layer_forward.1 = (bf16[1024,768]{1,0:T(8,128)(2,1)}, bf16[1024,768]{1,0:T(8,128)(2,1)}, bf16[1024,2304]{1,0:T(8,128)(2,1)}, bf16[6144,256]{1,0:T(8,128)(2,1)},...) custom-call(s32[1024]{0:T(1024)} %slots_ref.1, ...), custom_call_target="tpu_custom_call" | custom-call | tf_op jit(solution)/shard_map/layer_forward/pallas_call | solution.py:351
  82.2 114.0 %layer_backward.1 = (bf16[1024,768]{1,0:T(8,128)(2,1)}, bf16[1024,768]{1,0:T(8,128)(2,1)}, f32[16,128]{1,0:T(8,128)}, bf16[384,768]{1,0:T(8,128)(2,1)}, bf16[96,...) custom-call(bf16[1024,768]{1,0:T(8,128)(2,1)} %get-tuple-element.51.refs_0_, ...), custom_call_target="tpu_custom_call" | custom-call | tf_op jit(solution)/shard_map/layer_backward/pallas_call | solution.py:823
  196.2 7.5 %back_home.1 = (bf16[1024,768]{1,0:T(8,128)(2,1)}, bf16[1024,768]{1,0:T(8,128)(2,1)}, f32[96,2304]{1,0:T(8,128)}, f32[96,768]{1,0:T(8,128)}, f32[96,3072]{1,0:T(...) custom-call(s32[8,1024]{1,0:T(8,128)} %get-tuple-element.50.pos_ref,, ...), custom_call_target="tpu_custom_call" | custom-call | tf_op jit(solution)/shard_map/back_home/pallas_call | solution.py:894
